TPU v7x, 32 devices: a whole 2x2x4 slice. The times are simulated.
32 devices in a mesh: depth: 4 (over x, core), row: 4 (over z), col: 2 (over y).
Axes of the slice: x: 2, y: 2, z: 4, core: 2. Of those that a mesh axis runs over, the one named last changes fastest.
Arguments:
- density: float32 [4096, 4096], P('row', ('depth', 'col')), as said below
- pattern: int32 [64, 64], replicated, may hold values from 0 to 1, as said below
- filters: int32 [4, 64, 64], replicated, may hold values from 0 to 1, as said below
Outputs:
- purified: float32 [4096, 4096], P('row', ('depth', 'col'))
Inputs may be any that keep to these rules, and one draw needn't show every extreme that they name: density is symmetric. `pattern`: symmetric 0/1 block table with every diagonal block set. `filters`: each table is a symmetric 0/1 block table with every diagonal block set.
All inputs are finite; a program needn't handle non-finite values.
Results may differ from a plain program's by a relative error of at most 0.007.
Values may be sent and summed in bfloat16 or wider, within the bound.
A program may use at most 64 MiB of HBM per device.

v0:
```python
import jax
import jax.numpy as jnp
from jax import lax
from jax.sharding import PartitionSpec as P

BLK = 64
PURIFY = 2


def spread(value, axis, root):
    mine = lax.axis_index(axis) == root
    return lax.psum(jnp.where(mine, value, jnp.zeros_like(value)), axis)


def on_device(density, pattern, filters):
    rows_wide, seg_width = density.shape
    n_depth = lax.axis_size("depth")
    n_col = lax.axis_size("col")
    layer_index = lax.axis_index("depth")
    row_index = lax.axis_index("row")
    col_index = lax.axis_index("col")
    row_blocks = rows_wide // BLK
    seg_blocks = seg_width // BLK

    def full_mask(keep_table):
        row_strip = lax.dynamic_slice_in_dim(keep_table, row_index * row_blocks, row_blocks, 0)
        groups = row_strip.reshape(row_blocks, n_depth, n_col, seg_blocks)
        picked = lax.dynamic_slice_in_dim(groups, col_index, 1, 2)
        return picked.reshape(row_blocks, n_depth * seg_blocks).astype(jnp.float32)

    def own_mask(keep_table):
        return lax.dynamic_slice_in_dim(
            full_mask(keep_table), layer_index * seg_blocks, seg_blocks, 1
        )

    def apply_mask(values, keep_mask):
        row_count, col_count = keep_mask.shape
        shaped = values.reshape(row_count, BLK, col_count, BLK) * keep_mask[:, None, :, None]
        return shaped.reshape(values.shape)

    def multiply(left_tile, right_side):
        return jnp.dot(
            lax.all_gather(left_tile, "col", axis=1, tiled=True),
            right_side,
            preferred_element_type=jnp.float32,
        )

    def share_layers(partial_sum):
        return lax.psum_scatter(partial_sum, "depth", scatter_dimension=1, tiled=True)

    start_matrix = apply_mask(density, own_mask(pattern))
    current = start_matrix
    for round_index in range(PURIFY):
        operand = current.astype(jnp.bfloat16)
        right_side = spread(
            lax.all_gather(operand, "depth", axis=1, tiled=True), "row", layer_index
        )
        square = apply_mask(
            share_layers(multiply(operand, right_side)), own_mask(filters[2 * round_index])
        )
        cubic = apply_mask(
            share_layers(multiply(square.astype(jnp.bfloat16), right_side)),
            own_mask(filters[2 * round_index + 1]),
        )
        current = 3.0 * square - 2.0 * cubic
    return current


def solution(mesh):
    return jax.shard_map(
        on_device,
        mesh=mesh,
        in_specs=(P("row", ("depth", "col")), P(), P()),
        out_specs=P("row", ("depth", "col")),
        check_vma=False,
    )
```

profile of v0, /device:TPU:1, one launch (start us, length us, event | category | flops | bytes accessed | tf_op | source)
XLA Modules:
  0.0 889.3 jit_solution(13428316623293829066)
XLA Ops:
  9.8 3.4 mul.84
  13.2 2.9 multiply_convert_fusion
  16.9 36.3 %all-gather.9.cloned.1.call-done = bf16[1024,2048]{1,0:T(8,128)(2,1)} async-done(((bf16[1024,512]{1,0:T(8,128)(2,1)}), bf16[1024,2048]{1,0:T(8,128)(2,1)}) %all-gather.9.cloned.1.call-update) | async-done | bytes 4194320 | tf_op jit(solution)/shard_map/all_gather | solution.py:56
  55.6 31.9 %all-gather.7.cloned.1.call-done = bf16[1024,1024]{1,0:T(8,128)(2,1)} async-done(((bf16[1024,512]{1,0:T(8,128)(2,1)}), bf16[1024,1024]{1,0:T(8,128)(2,1)}) %all-gather.7.cloned.1.call-update) | async-done | bytes 2097168 | tf_op jit(solution)/shard_map/all_gather | solution.py:43
  87.5 157.4 %all-reduce.3.cloned.1.call-done = bf16[1024,2048]{1,0:T(8,128)(2,1)} async-done(((bf16[1024,2048]{1,0:T(8,128)(2,1)}), bf16[1024,2048]{1,0:T(8,128)(2,1)}) %all-reduce.3.cloned.1.call-update) | async-done | bytes 4194320 | tf_op jit(solution)/shard_map/psum | solution.py:12
  244.9 10.6 %fusion.1 = f32[1024,2048]{1,0:T(8,128)} fusion(bf16[1024,1024]{1,0:T(8,128)(2,1)} %all-gather.7.cloned.1.call-done, bf16[1024,2048]{1,0:T(8,128)(2,1)} %all-reduce.3.cloned.1.call-done), kind=kOutput, calls=%fused_computation.23 | convolution fusion | flops 4294967296 | bytes 14680064 | tf_op jit(solution)/shard_map/dot_general | solution.py:42
  258.9 3.5 mul.87
  262.4 64.0 %reduce-scatter.5.cloned.1.call-done = f32[1024,512]{1,0:T(8,128)} async-done(((f32[1024,2048]{1,0:T(8,128)}), f32[1024,512]{1,0:T(8,128)}) %reduce-scatter.5.cloned.1.call-update) | async-done | bytes 2097168 | tf_op jit(solution)/shard_map/reduce_scatter | solution.py:49
  329.4 33.2 %all-gather.11.cloned.1.call-done = bf16[1024,1024]{1,0:T(8,128)(2,1)} async-done(((bf16[1024,512]{1,0:T(8,128)(2,1)}), bf16[1024,1024]{1,0:T(8,128)(2,1)}) %all-gather.11.cloned.1.call-update) | async-done | bytes 2097168 | tf_op jit(solution)/shard_map/all_gather | solution.py:43
  362.6 10.6 %fusion.2 = f32[1024,2048]{1,0:T(8,128)} fusion(bf16[1024,1024]{1,0:T(8,128)(2,1)} %all-gather.11.cloned.1.call-done, bf16[1024,2048]{1,0:T(8,128)(2,1)} %all-reduce.3.cloned.1.call-done), kind=kOutput, calls=%fused_computation.24 | convolution fusion | flops 4294967296 | bytes 14680064 | tf_op jit(solution)/shard_map/dot_general | solution.py:42
  375.9 4.9 mul.91
  380.9 64.2 %reduce-scatter.7.cloned.1.call-done = f32[1024,512]{1,0:T(8,128)} async-done(((f32[1024,2048]{1,0:T(8,128)}), f32[1024,512]{1,0:T(8,128)}) %reduce-scatter.7.cloned.1.call-update) | async-done | bytes 2097168 | tf_op jit(solution)/shard_map/reduce_scatter | solution.py:49
  445.1 4.9 subtract_convert_fusion
  450.9 34.2 %all-gather.15.cloned.1.call-done = bf16[1024,2048]{1,0:T(8,128)(2,1)} async-done(((bf16[1024,512]{1,0:T(8,128)(2,1)}), bf16[1024,2048]{1,0:T(8,128)(2,1)}) %all-gather.15.cloned.1.call-update) | async-done | bytes 4194320 | tf_op jit(solution)/shard_map/all_gather | solution.py:56
  487.4 32.1 %all-gather.13.cloned.1.call-done = bf16[1024,1024]{1,0:T(8,128)(2,1)} async-done(((bf16[1024,512]{1,0:T(8,128)(2,1)}), bf16[1024,1024]{1,0:T(8,128)(2,1)}) %all-gather.13.cloned.1.call-update) | async-done | bytes 2097168 | tf_op jit(solution)/shard_map/all_gather | solution.py:43
  519.5 157.5 %all-reduce.5.cloned.1.call-done = bf16[1024,2048]{1,0:T(8,128)(2,1)} async-done(((bf16[1024,2048]{1,0:T(8,128)(2,1)}), bf16[1024,2048]{1,0:T(8,128)(2,1)}) %all-reduce.5.cloned.1.call-update) | async-done | bytes 4194320 | tf_op jit(solution)/shard_map/psum | solution.py:12
  677.0 10.6 %fusion.3 = f32[1024,2048]{1,0:T(8,128)} fusion(bf16[1024,1024]{1,0:T(8,128)(2,1)} %all-gather.13.cloned.1.call-done, bf16[1024,2048]{1,0:T(8,128)(2,1)} %all-reduce.5.cloned.1.call-done), kind=kOutput, calls=%fused_computation.25 | convolution fusion | flops 4294967296 | bytes 14680064 | tf_op jit(solution)/shard_map/dot_general | solution.py:42
  690.1 3.8 mul.95
  694.0 64.6 %reduce-scatter.9.cloned.1.call-done = f32[1024,512]{1,0:T(8,128)} async-done(((f32[1024,2048]{1,0:T(8,128)}), f32[1024,512]{1,0:T(8,128)}) %reduce-scatter.9.cloned.1.call-update) | async-done | bytes 2097168 | tf_op jit(solution)/shard_map/reduce_scatter | solution.py:49
  761.7 33.0 %all-gather.17.cloned.1.call-done = bf16[1024,1024]{1,0:T(8,128)(2,1)} async-done(((bf16[1024,512]{1,0:T(8,128)(2,1)}), bf16[1024,1024]{1,0:T(8,128)(2,1)}) %all-gather.17.cloned.1.call-update) | async-done | bytes 2097168 | tf_op jit(solution)/shard_map/all_gather | solution.py:43
  794.7 10.6 %fusion.4 = f32[1024,2048]{1,0:T(8,128)} fusion(bf16[1024,1024]{1,0:T(8,128)(2,1)} %all-gather.17.cloned.1.call-done, bf16[1024,2048]{1,0:T(8,128)(2,1)} %all-reduce.5.cloned.1.call-done), kind=kOutput, calls=%fused_computation.26 | convolution fusion | flops 4294967296 | bytes 14680064 | tf_op jit(solution)/shard_map/dot_general | solution.py:42
  807.8 4.9 mul.99
  812.7 64.5 %reduce-scatter.11.cloned.1.call-done = f32[1024,512]{1,0:T(8,128)} async-done(((f32[1024,2048]{1,0:T(8,128)}), f32[1024,512]{1,0:T(8,128)}) %reduce-scatter.11.cloned.1.call-update) | async-done | bytes 2097168 | tf_op jit(solution)/shard_map/reduce_scatter | solution.py:49
  877.2 5.2 multiply_subtract_fusion
  (63 shorter events, 26.7 us)
Async XLA Ops:
  6.5 0.8 copy-start
  6.5 46.7 %all-gather.9.cloned.1.call-start = ((), (), s32[]{:S(2)}) async-start(), calls=%async_computation.5 | async-start | bytes 5242880 | tf_op jit(solution)/shard_map/all_gather | solution.py:56
  16.1 71.4 %all-gather.7.cloned.1.call-start = ((), (), s32[]{:S(2)}) async-start(), calls=%async_computation.4 | async-start | bytes 3145728 | tf_op jit(solution)/shard_map/all_gather | solution.py:43
  16.9 228.0 %all-reduce.3.cloned.1.call-start = ((), (), s32[]{:S(2)}) async-start(), calls=%async_computation.6 | async-start | bytes 8388608 | tf_op jit(solution)/shard_map/psum | solution.py:12
  55.6 270.8 %reduce-scatter.5.cloned.1.call-start = ((), (), s32[]{:S(2)}) async-start(), calls=%async_computation.7 | async-start | bytes 10485760 | tf_op jit(solution)/shard_map/reduce_scatter | solution.py:49
  255.5 0.9 copy-start.2
  255.5 107.1 %all-gather.11.cloned.1.call-start = ((), (), s32[]{:S(2)}) async-start(), calls=%async_computation.8 | async-start | bytes 3145728 | tf_op jit(solution)/shard_map/all_gather | solution.py:43
  329.3 115.8 %reduce-scatter.7.cloned.1.call-start = ((), (), s32[]{:S(2)}) async-start(), calls=%async_computation.9 | async-start | bytes 10485760 | tf_op jit(solution)/shard_map/reduce_scatter | solution.py:49
  373.2 111.9 %all-gather.15.cloned.1.call-start = ((), (), s32[]{:S(2)}) async-start(), calls=%async_computation.11 | async-start | bytes 5242880 | tf_op jit(solution)/shard_map/all_gather | solution.py:56
  450.1 69.4 %all-gather.13.cloned.1.call-start = ((), (), s32[]{:S(2)}) async-start(), calls=%async_computation.10 | async-start | bytes 3145728 | tf_op jit(solution)/shard_map/all_gather | solution.py:43
  450.8 226.2 %all-reduce.5.cloned.1.call-start = ((), (), s32[]{:S(2)}) async-start(), calls=%async_computation.12 | async-start | bytes 8388608 | tf_op jit(solution)/shard_map/psum | solution.py:12
  487.4 271.2 %reduce-scatter.9.cloned.1.call-start = ((), (), s32[]{:S(2)}) async-start(), calls=%async_computation.13 | async-start | bytes 10485760 | tf_op jit(solution)/shard_map/reduce_scatter | solution.py:49
  687.6 107.1 %all-gather.17.cloned.1.call-start = ((), (), s32[]{:S(2)}) async-start(), calls=%async_computation.14 | async-start | bytes 3145728 | tf_op jit(solution)/shard_map/all_gather | solution.py:43
  761.4 115.8 %reduce-scatter.11.cloned.1.call-start = ((), (), s32[]{:S(2)}) async-start(), calls=%async_computation.15 | async-start | bytes 10485760 | tf_op jit(solution)/shard_map/reduce_scatter | solution.py:49
  877.2 5.2 copy-start.1
Sparse Core Ops, SparseCore 0:
  16.2 36.9 all-gather.8
  54.8 32.7 all-gather.6
  89.9 154.9 all-reduce.2
  255.6 70.7 reduce-scatter.4
  329.5 33.1 all-gather.10
  373.3 71.7 reduce-scatter.6
  450.2 34.8 all-gather.14
  486.7 32.7 all-gather.12
  522.0 154.9 all-reduce.4
  687.7 70.7 reduce-scatter.8
  761.6 33.1 all-gather.16
  805.4 71.7 reduce-scatter.10
where the time goes:
time: 891 us; the launch traced here: 889 us
  waiting for transfers between devices  775 us (87%)
  matrix products  42.3 us (5%)
  local copies, waits for them, and re-layouts  34.5 us (4%)
  other arithmetic  23.4 us (3%)
  between operations  13.7 us (2%)
    psum x2, waiting for transfers between devices, spread(): return lax.psum(jnp.where(mine, value, jnp.zeros_like(value)), axis)  315 us
    reduce_scatter x4, waiting for transfers between devices, share_layers(): lax.psum_scatter(partial_sum, 'depth', scatter_dimension=1, tiled=True)  257 us
    all_gather x4, waiting for transfers between devices, multiply(): lax.all_gather(left_tile, 'col', axis=1, tiled=True)  130 us
    all_gather x2, waiting for transfers between devices, on_device(): lax.all_gather(operand, 'depth', axis=1, tiled=True)  70.6 us
    dot_general x4, matrix products, multiply(): jnp.dot(lax.all_gather(left_tile, 'col', axis=1, tiled=True), right_side,...  42.3 us
    mul x10, local copies, waits for them, and re-layouts, apply_mask(): values.reshape(row_count, BLK, col_count, BLK) * keep_mask[:, None, :, None]  32.1 us
  transfers between devices with their start and end apart: 12, of which 12 were waited for; matrix products, arithmetic and copies ran while one was open for 4% of the time, Pallas kernels for 0%

commit v1 on v0

v1 whole, which is shorter than its diff:
```python
import functools

import jax
import jax.numpy as jnp
from jax import lax
from jax.experimental import pallas as pl
from jax.experimental.pallas import tpu as pltpu
from jax.sharding import PartitionSpec as P

BLK = 64
PURIFY = 2
CORES = 2
MESH = pl.DeviceIdType.MESH


def kernel(dims, dens, tabs, out, a_row, a_col, s_row, sq, acc, mask,
           z_send, z_recv, a_send, a_recv, af_send, af_recv,
           s_send, s_recv, sf_send, sf_recv):
    nd, nr, nc, h, w, cw, tm = dims
    Q = w // cw
    nx = nd // CORES
    m = h // w
    rb, sb = h // BLK, w // BLK
    d, r, c = lax.axis_index("depth"), lax.axis_index("row"), lax.axis_index("col")
    x, core = d // CORES, d % CORES
    sib = x * CORES + (1 - core)
    me = d * nc + c
    peers = [(px, pc) for px in range(nx) for pc in range(nc) if px or pc]

    def dev(dd, rr, cc):
        return (dd, rr, cc)

    def peer_to(p):
        px, pc = peers[p]
        return ((x + px) % nx) * CORES + core, (c + pc) % nc

    def peer_from(p, k):
        px, pc = peers[p]
        return ((x + nx - px) % nx) * CORES + k, (c + nc - pc) % nc

    bar = pltpu.get_barrier_semaphore()
    for p in range(len(peers)):
        dd, cc = peer_to(p)
        pl.semaphore_signal(bar, inc=1, device_id=dev(dd, r, cc), device_id_type=MESH)
    pl.semaphore_signal(bar, inc=1, device_id=dev(sib, r, c), device_id_type=MESH)

    @pl.when(r > 0)
    def _():
        pl.semaphore_signal(bar, inc=1, device_id=dev(d, r - 1, c), device_id_type=MESH)

    @pl.when(r < nr - 1)
    def _():
        pl.semaphore_signal(bar, inc=1, device_id=dev(d, r + 1, c), device_id_type=MESH)

    tb = tm // BLK
    slot = lax.broadcasted_iota(jnp.int32, (h // tm * 8, tabs.shape[1]), 0)
    r_pick = (slot // 8 * tb + slot % 8 + r * rb
              == lax.broadcasted_iota(jnp.int32, (h // tm * 8, tabs.shape[1]), 1)).astype(jnp.float32)
    c_pick = ((lax.broadcasted_iota(jnp.int32, (tabs.shape[2], w), 1) // BLK + me * sb)
              == lax.broadcasted_iota(jnp.int32, (tabs.shape[2], w), 0)).astype(jnp.float32)
    for k in range(tabs.shape[0]):
        rows = jnp.dot(r_pick, tabs[k].astype(jnp.float32), preferred_element_type=jnp.float32)
        mask[k] = jnp.dot(rows, c_pick, preferred_element_type=jnp.float32)

    def tile_mask(k, t, q):
        mk = mask[k, pl.ds(pl.multiple_of(t * 8, 8), 8), q * cw:(q + 1) * cw][:tb]
        return jnp.broadcast_to(mk[:, None, :], (tb, BLK, cw)).reshape(tm, cw)

    def rows_of(t):
        return pl.ds(pl.multiple_of(t * tm, tm), tm)

    @pl.loop(0, h // tm)
    def _(t):
        for q in range(Q):
            v = (dens[rows_of(t), q * cw:(q + 1) * cw] * tile_mask(0, t, q)).astype(jnp.bfloat16)
            a_col[0, r, q, rows_of(t), :] = v
            a_row[0, me, q, rows_of(t), :] = v

    near = jnp.minimum(r, 1) + jnp.minimum(nr - 1 - r, 1)
    for n in range(3):
        @pl.when(near == n)
        def _():
            pl.semaphore_wait(bar, len(peers) + 1 + n)

    def z_copy(s, q, src, up):
        ref = a_col.at[s, src, q]
        return pltpu.make_async_remote_copy(
            src_ref=ref, dst_ref=ref, send_sem=z_send.at[s, q, src, up],
            recv_sem=z_recv.at[s, q, src],
            device_id=dev(d, r + 1 if up else r - 1, c), device_id_type=MESH)

    def z_own(s, q, op):
        @pl.when(r < nr - 1)
        def _():
            getattr(z_copy(s, q, r, 1), op)()

        @pl.when(r > 0)
        def _():
            getattr(z_copy(s, q, r, 0), op)()

    def z_arrive(s, q, dist):
        @pl.when(r + dist < nr)
        def _():
            z_copy(s, q, r + dist, 1).wait_recv()

            @pl.when(r > 0)
            def _():
                z_copy(s, q, r + dist, 0).start()

        @pl.when(r - dist >= 0)
        def _():
            z_copy(s, q, r - dist, 0).wait_recv()

            @pl.when(r < nr - 1)
            def _():
                z_copy(s, q, r - dist, 1).start()

    def z_drain(s, q):
        z_own(s, q, "wait_send")
        for dist in range(1, nr - 1):
            @pl.when((r + dist < nr) & (r > 0))
            def _():
                z_copy(s, q, r + dist, 0).wait_send()

            @pl.when((r - dist >= 0) & (r < nr - 1))
            def _():
                z_copy(s, q, r - dist, 1).wait_send()

    def ac(ref, ss, rs, to):
        return pltpu.make_async_remote_copy(
            src_ref=ref, dst_ref=ref, send_sem=ss, recv_sem=rs,
            device_id=dev(to[0], r, to[1]), device_id_type=MESH)

    class Gather:
        def __init__(self, view, send, recv, fsend, frecv):
            self.view, self.send, self.recv = view, send, recv
            self.fsend, self.frecv = fsend, frecv

        def own(self, p):
            return ac(self.view(me), self.send(p), self.recv(p), peer_to(p))

        def got(self, p):
            dd, cc = peer_from(p, core)
            return ac(self.view(dd * nc + cc), self.send(p), self.recv(p), peer_to(p))

        def fwd(self, p):
            if p == len(peers):
                return ac(self.view(me), self.fsend(p), self.frecv(p), (sib, c))
            dd, cc = peer_from(p, core)
            return ac(self.view(dd * nc + cc), self.fsend(p), self.frecv(p), (sib, c))

        def fgot(self, p):
            if p == len(peers):
                dd, cc = sib, c
            else:
                dd, cc = peer_from(p, 1 - core)
            return ac(self.view(dd * nc + cc), self.fsend(p), self.frecv(p), (sib, c))

        def begin(self):
            for p in range(len(peers)):
                self.own(p).start()
            self.fwd(len(peers)).start()

        def relay(self):
            for p in range(len(peers)):
                self.got(p).wait_recv()
                self.fwd(p).start()

        def finish(self):
            for p in range(len(peers) + 1):
                self.fgot(p).wait_recv()

        def drain(self):
            for p in range(len(peers)):
                self.own(p).wait_send()
            for p in range(len(peers) + 1):
                self.fwd(p).wait_send()

    ga = [Gather(lambda j, s=s: a_row.at[s, j], lambda p, s=s: a_send.at[s, p],
                 lambda p, s=s: a_recv.at[s, p], lambda p, s=s: af_send.at[s, p],
                 lambda p, s=s: af_recv.at[s, p]) for s in range(PURIFY)]
    gs = [[Gather(lambda j, s=s, q=q: s_row.at[s, j, q], lambda p, s=s, q=q: s_send.at[s, q, p],
                  lambda p, s=s, q=q: s_recv.at[s, q, p], lambda p, s=s, q=q: sf_send.at[s, q, p],
                  lambda p, s=s, q=q: sf_recv.at[s, q, p]) for q in range(Q)] for s in range(PURIFY)]

    def square(s, q):
        @pl.loop(0, h // tm)
        def _(t):
            tot = None
            for j in range(nd * nc):
                for k in range(Q):
                    lo = (j % m) * w + k * cw
                    part = jnp.dot(a_row[s, j, k, rows_of(t), :],
                                   a_col[s, j // m, q, lo:lo + cw, :],
                                   preferred_element_type=jnp.float32)
                    tot = part if tot is None else tot + part
            tot = tot * tile_mask(2 * s + 1, t, q)
            sq[q, rows_of(t), :] = tot
            s_row[s, me, q, rows_of(t), :] = tot.astype(jnp.bfloat16)

    def cubic(s, k):
        @pl.loop(0, h // tm)
        def _(t):
            for q in range(Q):
                tot = None if k == 0 else acc[q, rows_of(t), :]
                for j in range(nd * nc):
                    lo = (j % m) * w + k * cw
                    part = jnp.dot(s_row[s, j, k, rows_of(t), :],
                                   a_col[s, j // m, q, lo:lo + cw, :],
                                   preferred_element_type=jnp.float32)
                    tot = part if tot is None else tot + part
                if k < Q - 1:
                    acc[q, rows_of(t), :] = tot
                else:
                    cur = 3.0 * sq[q, rows_of(t), :] - 2.0 * (tot * tile_mask(2 * s + 2, t, q))
                    if s < PURIFY - 1:
                        v = cur.astype(jnp.bfloat16)
                        a_col[s + 1, r, q, rows_of(t), :] = v
                        a_row[s + 1, me, q, rows_of(t), :] = v
                    else:
                        out[rows_of(t), q * cw:(q + 1) * cw] = cur

    for s in range(PURIFY):
        z_own(s, 0, "start")
        ga[s].begin()
        for q in range(Q):
            for dist in range(1, nr):
                z_arrive(s, q, dist)
                if q + 1 < Q and dist == min(2, nr - 1):
                    z_own(s, q + 1, "start")
            if q == 0:
                ga[s].relay()
                ga[s].finish()
            square(s, q)
            gs[s][q].begin()
        for k in range(Q):
            gs[s][k].relay()
            gs[s][k].finish()
            cubic(s, k)
    for s in range(PURIFY):
        ga[s].drain()
        for q in range(Q):
            z_drain(s, q)
            gs[s][q].drain()


def on_device(dims, density, pattern, filters):
    nd, nr, nc, h, w, cw, tm = dims
    Q = w // cw
    J = nd * nc
    n_peers = J // CORES - 1
    tabs = jnp.concatenate([pattern[None], filters], 0)
    dma = pltpu.SemaphoreType.DMA
    return pl.pallas_call(
        functools.partial(kernel, dims),
        out_shape=jax.ShapeDtypeStruct((h, w), jnp.float32),
        in_specs=[pl.BlockSpec(memory_space=pltpu.VMEM)] * 2,
        out_specs=pl.BlockSpec(memory_space=pltpu.VMEM),
        scratch_shapes=[
            pltpu.VMEM((PURIFY, J, Q, h, cw), jnp.bfloat16),
            pltpu.VMEM((PURIFY, nr, Q, h, cw), jnp.bfloat16),
            pltpu.VMEM((PURIFY, J, Q, h, cw), jnp.bfloat16),
            pltpu.VMEM((Q, h, cw), jnp.float32),
            pltpu.VMEM((Q, h, cw), jnp.float32),
            pltpu.VMEM((2 * PURIFY + 1, h // tm * 8, w), jnp.float32),
            dma((PURIFY, Q, nr, 2)), dma((PURIFY, Q, nr)),
            dma((PURIFY, n_peers)), dma((PURIFY, n_peers)),
            dma((PURIFY, n_peers + 1)), dma((PURIFY, n_peers + 1)),
            dma((PURIFY, Q, n_peers)), dma((PURIFY, Q, n_peers)),
            dma((PURIFY, Q, n_peers + 1)), dma((PURIFY, Q, n_peers + 1)),
        ],
        compiler_params=pltpu.CompilerParams(
            collective_id=0, has_side_effects=True, vmem_limit_bytes=62 * 2 ** 20),
    )(density, tabs)


def solution(mesh):
    nd, nr, nc = mesh.shape["depth"], mesh.shape["row"], mesh.shape["col"]

    def run(density, pattern, filters):
        h, w = density.shape
        cw = 256 if w % 256 == 0 else w
        tm = 256 if h % 256 == 0 else h
        return on_device((nd, nr, nc, h, w, cw, tm), density, pattern, filters)

    return jax.shard_map(
        run,
        mesh=mesh,
        in_specs=(P("row", ("depth", "col")), P(), P()),
        out_specs=P("row", ("depth", "col")),
        check_vma=False,
    )
```

time: 891 us -> 230 us (0.26)
  waiting for transfers between devices: 775 us -> 0 us
  Pallas kernels: 0 us -> 226 us
  matrix products: 42.3 us -> 0 us
  local copies, waits for them, and re-layouts: 34.5 us -> 3.08 us
  other arithmetic: 23.4 us -> 1.59 us
  between operations: 13.7 us -> 0.01 us
    psum x2 -> x0, waiting for transfers between devices: 315 us -> none  [spread(): return lax.psum(jnp.where(mine, value, jnp.zeros_like(value)), axis)]
    reduce_scatter x4 -> x0, waiting for transfers between devices: 257 us -> none  [share_layers(): lax.psum_scatter(partial_sum, 'depth', scatter_dimension=1, tiled=True)]
    pallas_call x0 -> x1, Pallas kernels: none -> 226 us  [on_device(): pl.pallas_call(functools.partial(kernel, dims), out_shape=jax.ShapeDtypeS...]
    all_gather x6 -> x0, waiting for transfers between devices: 201 us -> none  [the longest x4 130 us: multiply(): lax.all_gather(left_tile, 'col', axis=1, tiled=True)]
    dot_general x4 -> x0, matrix products: 42.3 us -> none  [multiply(): jnp.dot(lax.all_gather(left_tile, 'col', axis=1, tiled=True), right_side,...]
    mul x10 -> x0, local copies, waits for them, and re-layouts: 32.1 us -> none  [apply_mask(): values.reshape(row_count, BLK, col_count, BLK) * keep_mask[:, None, :, None]]
    convert_element_type x9 -> x0, other arithmetic: 13.7 us -> none  [the longest x2 7.84 us: on_device(): operand = current.astype(jnp.bfloat16)]
  transfers between devices with their start and end apart: 12 -> 0, of which waited for: 12 -> 0; matrix products, arithmetic and copies ran while one was open for 4% -> 0% of each run, Pallas kernels for 0% -> 0%
where the time goes in v1:
time: 230 us
  Pallas kernels  226 us (98%)
  local copies, waits for them, and re-layouts  3.08 us (1%)
    pallas_call x1, Pallas kernels, on_device(): pl.pallas_call(functools.partial(kernel, dims), out_shape=jax.ShapeDtypeS...  226 us

profile of v1, /device:TPU:1, one launch (start us, length us, event | category | flops | bytes accessed | tf_op | source)
XLA Modules:
  0.0 230.3 jit_solution(15038495969738623295)
XLA Ops:
  0.0 1.6 pad_add_fusion.tabs
  1.6 225.6 %shard_map.37 = f32[1024,512]{1,0:T(8,128)} custom-call(f32[1024,512]{1,0:T(8,128)} %dens.1, s32[5,64,64]{2,1,0:T(8,128)} %pad_add_fusion.tabs), custom_call_target="tpu_custom_call" | custom-call | tf_op jit(solution)/shard_map/pallas_call | solution.py:254
  227.2 3.1 %copy.5 = f32[1024,512]{1,0:T(8,128)} copy(f32[1024,512]{1,0:T(8,128)} %shard_map.37) | data formatting | bytes 4194304

commit v2 on v1

v2 whole, which is shorter than its diff:
```python
import functools

import jax
import jax.numpy as jnp
from jax import lax
from jax.experimental import pallas as pl
from jax.experimental.pallas import tpu as pltpu
from jax.sharding import PartitionSpec as P

BLK = 64
PURIFY = 2
CORES = 2
LANES = 128
MESH = pl.DeviceIdType.MESH


def kernel(dims, dens, tabs, out, a_row, a_col, s_row, sq, acc, mask,
           z_send, z_recv, a_send, a_recv, af_send, af_recv,
           s_send, s_recv, sf_send, sf_recv):
    nd, nr, nc, h, w, tm, cuts = dims
    Q = len(cuts)
    G = w // LANES
    nx = nd // CORES
    m = h // w
    rb, sb = h // BLK, w // BLK
    d, r, c = lax.axis_index("depth"), lax.axis_index("row"), lax.axis_index("col")
    x, core = d // CORES, d % CORES
    sib = x * CORES + (1 - core)
    me = d * nc + c
    peers = [(px, pc) for px in range(nx) for pc in range(nc) if px or pc]
    direct = [p for p, (px, pc) in enumerate(peers) if not (px and pc)]
    bent = [p for p, (px, pc) in enumerate(peers) if px and pc]

    def dev(dd, rr, cc):
        return (dd, rr, cc)

    def peer_to(p):
        px, pc = peers[p]
        return ((x + px) % nx) * CORES + core, (c + pc) % nc

    def peer_from(p, k):
        px, pc = peers[p]
        return ((x + nx - px) % nx) * CORES + k, (c + nc - pc) % nc

    bar = pltpu.get_barrier_semaphore()
    for p in direct:
        dd, cc = peer_to(p)
        pl.semaphore_signal(bar, inc=1, device_id=dev(dd, r, cc), device_id_type=MESH)
    pl.semaphore_signal(bar, inc=1, device_id=dev(sib, r, c), device_id_type=MESH)

    @pl.when(r > 0)
    def _():
        pl.semaphore_signal(bar, inc=1, device_id=dev(d, r - 1, c), device_id_type=MESH)

    @pl.when(r < nr - 1)
    def _():
        pl.semaphore_signal(bar, inc=1, device_id=dev(d, r + 1, c), device_id_type=MESH)

    tb = tm // BLK
    slot = lax.broadcasted_iota(jnp.int32, (h // tm * 8, tabs.shape[1]), 0)
    r_pick = (slot // 8 * tb + slot % 8 + r * rb
              == lax.broadcasted_iota(jnp.int32, (h // tm * 8, tabs.shape[1]), 1)).astype(jnp.float32)
    c_pick = ((lax.broadcasted_iota(jnp.int32, (tabs.shape[2], w), 1) // BLK + me * sb)
              == lax.broadcasted_iota(jnp.int32, (tabs.shape[2], w), 0)).astype(jnp.float32)
    for k in range(tabs.shape[0]):
        rows = jnp.dot(r_pick, tabs[k].astype(jnp.float32), preferred_element_type=jnp.float32)
        mask[k] = jnp.dot(rows, c_pick, preferred_element_type=jnp.float32)

    def tile_mask(k, t, g0, g1):
        n = (g1 - g0) * LANES
        mk = mask[k, pl.ds(pl.multiple_of(t * 8, 8), 8), g0 * LANES:g1 * LANES][:tb]
        return jnp.broadcast_to(mk[:, None, :], (tb, BLK, n)).reshape(tm, n)

    def rows_of(t):
        return pl.ds(pl.multiple_of(t * tm, tm), tm)

    @pl.loop(0, h // tm)
    def _(t):
        for g in range(G):
            v = (dens[rows_of(t), g * LANES:(g + 1) * LANES] * tile_mask(0, t, g, g + 1)).astype(jnp.bfloat16)
            a_col[0, r, g, rows_of(t), :] = v
            a_row[0, me, g, rows_of(t), :] = v

    near = jnp.minimum(r, 1) + jnp.minimum(nr - 1 - r, 1)
    for n in range(3):
        @pl.when(near == n)
        def _():
            pl.semaphore_wait(bar, len(direct) + 1 + n)

    def z_copy(s, q, src, up):
        ref = a_col.at[s, src, cuts[q][0]:cuts[q][1]]
        return pltpu.make_async_remote_copy(
            src_ref=ref, dst_ref=ref, send_sem=z_send.at[s, q, src, up],
            recv_sem=z_recv.at[s, q, src],
            device_id=dev(d, r + 1 if up else r - 1, c), device_id_type=MESH)

    def z_own(s, q, op):
        @pl.when(r < nr - 1)
        def _():
            getattr(z_copy(s, q, r, 1), op)()

        @pl.when(r > 0)
        def _():
            getattr(z_copy(s, q, r, 0), op)()

    def z_arrive(s, q, dist):
        @pl.when(r + dist < nr)
        def _():
            z_copy(s, q, r + dist, 1).wait_recv()

            @pl.when(r > 0)
            def _():
                z_copy(s, q, r + dist, 0).start()

        @pl.when(r - dist >= 0)
        def _():
            z_copy(s, q, r - dist, 0).wait_recv()

            @pl.when(r < nr - 1)
            def _():
                z_copy(s, q, r - dist, 1).start()

    def z_drain(s, q):
        z_own(s, q, "wait_send")
        for dist in range(1, nr - 1):
            @pl.when((r + dist < nr) & (r > 0))
            def _():
                z_copy(s, q, r + dist, 0).wait_send()

            @pl.when((r - dist >= 0) & (r < nr - 1))
            def _():
                z_copy(s, q, r - dist, 1).wait_send()

    def ac(ref, ss, rs, to):
        return pltpu.make_async_remote_copy(
            src_ref=ref, dst_ref=ref, send_sem=ss, recv_sem=rs,
            device_id=dev(to[0], r, to[1]), device_id_type=MESH)

    class Gather:
        def __init__(self, view, send, recv, fsend, frecv):
            self.view, self.send, self.recv = view, send, recv
            self.fsend, self.frecv = fsend, frecv

        def block(self, p, k):
            dd, cc = peer_from(p, k)
            return self.view(dd * nc + cc)

        def half(self, dd, cc, i):
            return self.view(dd * nc + cc).at[:, i * (h // 2):(i + 1) * (h // 2), :]

        def own(self, p):
            return ac(self.view(me), self.send(p, 0), self.recv(p, 0), peer_to(p))

        def got(self, p, i=None):
            if i is None:
                return ac(self.block(p, core), self.send(p, 0), self.recv(p, 0), peer_to(p))
            dd, cc = peer_from(p, core)
            return ac(self.half(dd, cc, i), self.send(p, i), self.recv(p, i), peer_to(p))

        def turn(self, p, i):
            px, pc = peers[p]
            if i == 0:
                ref = self.half(((x + nx - px) % nx) * CORES + core, c, 0)
                to = (d, (c + pc) % nc)
            else:
                ref = self.half(d, (c + nc - pc) % nc, 1)
                to = (((x + px) % nx) * CORES + core, c)
            return ac(ref, self.send(p, i), self.recv(p, i), to)

        def fwd(self, p):
            ref = self.view(me) if p == len(peers) else self.block(p, core)
            return ac(ref, self.fsend(p), self.frecv(p), (sib, c))

        def fgot(self, p):
            ref = self.view(sib * nc + c) if p == len(peers) else self.block(p, 1 - core)
            return ac(ref, self.fsend(p), self.frecv(p), (sib, c))

        def begin(self):
            for p in direct:
                self.own(p).start()
            self.fwd(len(peers)).start()

        def hop(self):
            for q in direct:
                self.got(q).wait_recv()
                for p in bent:
                    if peers[q] == (peers[p][0], 0):
                        self.turn(p, 0).start()
                    if peers[q] == (0, peers[p][1]):
                        self.turn(p, 1).start()
            for q in direct:
                self.fwd(q).start()

        def relay(self):
            for p in bent:
                self.got(p, 0).wait_recv()
                self.got(p, 1).wait_recv()
                self.fwd(p).start()

        def finish(self):
            for p in range(len(peers) + 1):
                self.fgot(p).wait_recv()

        def drain(self):
            for p in direct:
                self.own(p).wait_send()
            for p in bent:
                self.turn(p, 0).wait_send()
                self.turn(p, 1).wait_send()
            for p in range(len(peers) + 1):
                self.fwd(p).wait_send()

    ga = [Gather(lambda j, s=s: a_row.at[s, j], lambda p, i, s=s: a_send.at[s, p, i],
                 lambda p, i, s=s: a_recv.at[s, p, i], lambda p, s=s: af_send.at[s, p],
                 lambda p, s=s: af_recv.at[s, p]) for s in range(PURIFY)]
    gs = [[Gather(lambda j, s=s, q=q: s_row.at[s, j, cuts[q][0]:cuts[q][1]],
                  lambda p, i, s=s, q=q: s_send.at[s, q, p, i],
                  lambda p, i, s=s, q=q: s_recv.at[s, q, p, i],
                  lambda p, s=s, q=q: sf_send.at[s, q, p],
                  lambda p, s=s, q=q: sf_recv.at[s, q, p]) for q in range(Q)] for s in range(PURIFY)]

    def product(left, s, t, groups, g0, g1):
        cells = [(j, g) for j in range(nd * nc) for g in groups]
        tot = None
        for i in range(0, len(cells), 2):
            pair = cells[i:i + 2]
            lhs = jnp.concatenate([left[s, j, g, rows_of(t), :] for j, g in pair], axis=1)
            cols = []
            for n in range(g0, g1):
                los = [(j // m, (j % m) * w + g * LANES) for j, g in pair]
                if len(los) == 2 and los[1] == (los[0][0], los[0][1] + LANES):
                    cols.append(a_col[s, los[0][0], n, los[0][1]:los[0][1] + 2 * LANES, :])
                else:
                    cols.append(jnp.concatenate([a_col[s, b, n, lo:lo + LANES, :] for b, lo in los], axis=0))
            part = jnp.dot(lhs, jnp.concatenate(cols, axis=1), preferred_element_type=jnp.float32)
            tot = part if tot is None else tot + part
        return tot

    def square(s, q):
        g0, g1 = cuts[q]

        @pl.loop(0, h // tm)
        def _(t):
            tot = product(a_row, s, t, range(G), g0, g1) * tile_mask(2 * s + 1, t, g0, g1)
            sq[rows_of(t), g0 * LANES:g1 * LANES] = tot
            v = tot.astype(jnp.bfloat16)
            for g in range(g0, g1):
                s_row[s, me, g, rows_of(t), :] = v[:, (g - g0) * LANES:(g - g0 + 1) * LANES]

    def cubic(s, k, g0, g1):
        cols = slice(g0 * LANES, g1 * LANES)

        @pl.loop(0, h // tm)
        def _(t):
            tot = product(s_row, s, t, range(*cuts[k]), g0, g1)
            if k > 0:
                tot = tot + acc[rows_of(t), cols]
            if k < Q - 1:
                acc[rows_of(t), cols] = tot
                return
            cur = 3.0 * sq[rows_of(t), cols] - 2.0 * (tot * tile_mask(2 * s + 2, t, g0, g1))
            if s < PURIFY - 1:
                v = cur.astype(jnp.bfloat16)
                for g in range(g0, g1):
                    part = v[:, (g - g0) * LANES:(g - g0 + 1) * LANES]
                    a_col[s + 1, r, g, rows_of(t), :] = part
                    a_row[s + 1, me, g, rows_of(t), :] = part
            else:
                out[rows_of(t), cols] = cur

    wide = [(g, min(g + 2, G)) for g in range(0, G, 2)]
    for s in range(PURIFY):
        if s == 0:
            z_own(s, 0, "start")
        ga[s].begin()
        for q in range(Q):
            for dist in range(1, nr):
                z_arrive(s, q, dist)
                if q + 1 < Q and dist == min(2, nr - 1):
                    z_own(s, q + 1, "start")
                if q == 0 and dist == min(2, nr - 1):
                    ga[s].hop()
            if q == 0:
                ga[s].relay()
                ga[s].finish()
            if q >= 2:
                gs[s][q - 2].relay()
            if q >= 1:
                gs[s][q - 1].hop()
            square(s, q)
            gs[s][q].begin()
        if Q >= 2:
            gs[s][Q - 2].relay()
        for k in range(Q):
            if k == max(Q - 2, 0):
                gs[s][Q - 1].hop()
            if k == Q - 1:
                gs[s][k].relay()
            gs[s][k].finish()
            for i, (g0, g1) in enumerate(wide):
                cubic(s, k, g0, g1)
                if k == Q - 1 and s < PURIFY - 1 and g1 == cuts[0][1]:
                    z_own(s + 1, 0, "start")
    for s in range(PURIFY):
        ga[s].drain()
        for q in range(Q):
            z_drain(s, q)
            gs[s][q].drain()


def on_device(dims, density, pattern, filters):
    nd, nr, nc, h, w, tm, cuts = dims
    Q = len(cuts)
    G = w // LANES
    J = nd * nc
    n_peers = J // CORES - 1
    tabs = jnp.concatenate([pattern[None], filters], 0)
    dma = pltpu.SemaphoreType.DMA
    return pl.pallas_call(
        functools.partial(kernel, dims),
        out_shape=jax.ShapeDtypeStruct((h, w), jnp.float32),
        in_specs=[pl.BlockSpec(memory_space=pltpu.VMEM)] * 2,
        out_specs=pl.BlockSpec(memory_space=pltpu.VMEM),
        scratch_shapes=[
            pltpu.VMEM((PURIFY, J, G, h, LANES), jnp.bfloat16),
            pltpu.VMEM((PURIFY, nr, G, h, LANES), jnp.bfloat16),
            pltpu.VMEM((PURIFY, J, G, h, LANES), jnp.bfloat16),
            pltpu.VMEM((h, w), jnp.float32),
            pltpu.VMEM((h, w), jnp.float32),
            pltpu.VMEM((2 * PURIFY + 1, h // tm * 8, w), jnp.float32),
            dma((PURIFY, Q, nr, 2)), dma((PURIFY, Q, nr)),
            dma((PURIFY, n_peers, 2)), dma((PURIFY, n_peers, 2)),
            dma((PURIFY, n_peers + 1)), dma((PURIFY, n_peers + 1)),
            dma((PURIFY, Q, n_peers, 2)), dma((PURIFY, Q, n_peers, 2)),
            dma((PURIFY, Q, n_peers + 1)), dma((PURIFY, Q, n_peers + 1)),
        ],
        compiler_params=pltpu.CompilerParams(
            collective_id=0, has_side_effects=True, vmem_limit_bytes=62 * 2 ** 20),
    )(density, tabs)


def solution(mesh):
    nd, nr, nc = mesh.shape["depth"], mesh.shape["row"], mesh.shape["col"]

    def run(density, pattern, filters):
        h, w = density.shape
        tm = 256 if h % 256 == 0 else h
        groups = w // LANES
        cuts = [(g, g + 1) for g in range(groups)]
        if groups >= 4:
            cuts = [(g, g + 2) for g in range(0, groups - 2, 2)] + cuts[groups - 2:]
        return on_device((nd, nr, nc, h, w, tm, tuple(cuts)), density, pattern, filters)

    return jax.shard_map(
        run,
        mesh=mesh,
        in_specs=(P("row", ("depth", "col")), P(), P()),
        out_specs=P("row", ("depth", "col")),
        check_vma=False,
    )
```

time: 230 us -> 196 us (0.85)
  Pallas kernels: 226 us -> 191 us
    pallas_call x1, Pallas kernels: 226 us -> 191 us  [on_device(): pl.pallas_call(functools.partial(kernel, dims), out_shape=jax.ShapeDtypeS...]
where the time goes in v2:
time: 196 us
  Pallas kernels  191 us (97%)
  local copies, waits for them, and re-layouts  3.08 us (2%)
    pallas_call x1, Pallas kernels, on_device(): pl.pallas_call(functools.partial(kernel, dims), out_shape=jax.ShapeDtypeS...  191 us

profile of v2, /device:TPU:1, one launch (start us, length us, event | category | flops | bytes accessed | tf_op | source)
XLA Modules:
  0.0 195.9 jit_solution(223184990690256915)
XLA Ops:
  0.0 1.6 pad_add_fusion.tabs
  1.6 191.3 %shard_map.37 = f32[1024,512]{1,0:T(8,128)} custom-call(f32[1024,512]{1,0:T(8,128)} %dens.1, s32[5,64,64]{2,1,0:T(8,128)} %pad_add_fusion.tabs), custom_call_target="tpu_custom_call" | custom-call | tf_op jit(solution)/shard_map/pallas_call | solution.py:319
  192.9 3.1 %copy.5 = f32[1024,512]{1,0:T(8,128)} copy(f32[1024,512]{1,0:T(8,128)} %shard_map.37) | data formatting | bytes 4194304
